TPU v7x, 32 devices: a whole 2x2x4 slice. The times are simulated.
32 devices in a mesh: space: 8 (over z, x), member: 4 (over y, core).
Axes of the slice: x: 2, y: 2, z: 4, core: 2. Of those that a mesh axis runs over, the one named last changes fastest.
Arguments:
- fields: float32 [8, 16, 128, 256], P('member', 'space'), may hold values from -6 to 6
- velocity: float32 [16, 128, 256], P('space'), may hold values from 0.2 to 0.6
- building: int32 [16, 128, 256], P('space'), may hold values 0 or 1
- inflow_table: float32 [32, 128, 256], replicated, may hold values from -6 to 6
- inflow_index: int32 [8], P('member'), may hold values from 0 to 31
Outputs:
- fields_now: float32 [8, 16, 128, 256], P('member', 'space')
- r_factor: float32 [8, 8], replicated
All inputs are finite; a program needn't handle non-finite values. No bound on the sum of `building` on one device may be relied on, other than what follows from the above.
Results may differ from a plain program's by a relative error of at most 0.0003.
Values may be sent and summed in bfloat16 or wider, within the bound.
A program may use at most 64 MiB of HBM per device.

v0:
```python
import jax
import jax.numpy as jnp
from jax import lax
from jax.sharding import PartitionSpec as P

STEPS = 2


kappa_rate = 0.05
shrink_weight = 0.1
contract_dims = (((1,), (1,)), ((), ()))


def extended_2(block, sides, width):
    for axis, dim in sides:
        count = lax.axis_size(axis)
        forward = [(i, i + 1) for i in range(count - 1)]
        backward = [(target, source) for source, target in forward]
        low = lax.ppermute(
            lax.slice_in_dim(block, block.shape[dim] - width, None, axis=dim), axis, forward
        )
        high = lax.ppermute(lax.slice_in_dim(block, 0, width, axis=dim), axis, backward)
        block = jnp.concatenate([low, block, high], axis=dim)
    return block


def from_behind(block, axis, distance):
    devices = range(lax.axis_size(axis))
    route = [((i - distance) % len(devices), i) for i in devices]
    return lax.ppermute(block, axis, route)


def advance(extended, fluid_cells, courant):
    upwind = extended[:, :-2]
    centre = extended[:, 1:-1]
    downwind = extended[:, 2:]
    in_plane = (
        jnp.roll(centre, 1, 2)
        + jnp.roll(centre, -1, 2)
        + jnp.roll(centre, 1, 3)
        + jnp.roll(centre, -1, 3)
    )
    return fluid_cells * (
        centre
        + courant * (upwind - centre)
        + kappa_rate * (upwind + downwind + in_plane - 6.0 * centre)
    )


def local(fields, velocity, building, inflow_table, inflow_index):
    mem_dev = fields.shape[0]
    slab_depth = fields.shape[1]
    plane_rows = fields.shape[2]
    plane_cols = fields.shape[3]
    patterns = inflow_table.shape[0]
    fluid_cells = (1 - building).astype(jnp.float32)
    pattern_pick = (inflow_index[:, None] == jnp.arange(patterns, dtype=jnp.int32)[None, :]).astype(
        jnp.float32
    )
    inflow_plane = jnp.dot(
        pattern_pick,
        inflow_table.reshape(patterns, plane_rows * plane_cols),
        precision=lax.Precision.HIGHEST,
        preferred_element_type=jnp.float32,
    ).reshape(mem_dev, plane_rows, plane_cols)
    at_inflow = lax.axis_index("space") == 0
    fields_now = fields
    for sweep_index in range(STEPS):
        extended = extended_2(fields_now, (("space", 1),), 1)
        extended = extended.at[:, 0].set(jnp.where(at_inflow, inflow_plane, extended[:, 0]))
        fields_now = advance(extended, fluid_cells, velocity)
    groups = lax.axis_size("member")
    all_members = mem_dev * groups
    member_sum = jnp.sum(fields_now, 0)
    ensemble_mean = (
        lax.psum(member_sum.astype(jnp.bfloat16), "member").astype(jnp.float32) / all_members
    )
    anomaly = (
        (fields_now - ensemble_mean)
        .astype(jnp.bfloat16)
        .reshape(mem_dev, slab_depth * plane_rows * plane_cols)
    )
    my_group = lax.axis_index("member")
    cells_all = slab_depth * lax.axis_size("space") * plane_rows * plane_cols
    empty_rows = jnp.zeros((mem_dev, all_members), jnp.float32)

    def place(gram_tile, panel_piece, first_row):
        gram_block = lax.dot_general(
            anomaly, panel_piece, contract_dims, preferred_element_type=jnp.float32
        )
        return lax.dynamic_update_slice(
            gram_tile, gram_block, (jnp.int32(0), jnp.asarray(first_row))
        )

    gram_tile = place(empty_rows, anomaly, my_group * mem_dev)

    def turn(sweep_index, loop_state):
        tile_now, panel_held = loop_state
        panel_held = from_behind(panel_held, "member", 1)
        source = (my_group - sweep_index) % groups
        return (place(tile_now, panel_held, source * mem_dev), panel_held)

    gram_tile, panel_held = lax.fori_loop(1, groups, turn, (gram_tile, anomaly))
    gram_tile = gram_tile / cells_all
    summed = lax.psum(gram_tile, "space")
    gram_full = lax.all_gather(summed, "member", axis=0, tiled=True)
    r_factor = jnp.linalg.cholesky(
        gram_full + shrink_weight * jnp.eye(all_members, dtype=jnp.float32)
    ).T
    return (fields_now, r_factor)


def solution(mesh):
    placed = (
        P("member", "space", None, None),
        P("space", None, None),
        P("space", None, None),
        P(),
        P("member"),
    )
    return jax.shard_map(
        local,
        mesh=mesh,
        in_specs=placed,
        out_specs=(P("member", "space", None, None), P()),
        check_vma=False,
    )
```

profile of v0, /device:TPU:0, one launch (start us, length us, event | category | flops | bytes accessed | tf_op | source)
XLA Modules:
  0.0 151.2 jit_solution(6526579312249673913)
XLA Ops:
  7.2 0.0 copy-start.1
  7.2 0.0 all-reduce.2.cloned.1.call-start
  7.2 1.4 copy.24
  8.7 0.2 fusion.33
  8.9 4.9 %collective-permute-start.1 = (f32[2,1,128,256]{3,0,2,1:T(2,128)S(1)}, f32[2,1,128,256]{3,0,2,1:T(2,128)S(1)}, u32[]{:S(2)}, u32[]{:S(2)}) collective-permute-start(f32[2,1,128,256]{3,0,2,1:T(2,128)S(1)} %get-tuple-element.196), channel_id=1, source_target_pairs={{0,4},{4,8},{8,12},{12,16},{16,20},{20,24},{24,28},{1,5},{5,9},{9,... | collective-permute-start | bytes 786440 | tf_op jit(solution)/shard_map/ppermute | solution.py:19
  13.7 1.3 collective-permute-start.2
  15.0 1.0 subtract_convert_fusion.1
  16.0 8.9 %collective-permute-done.1 = f32[2,1,128,256]{3,0,2,1:T(2,128)S(1)} collective-permute-done((f32[2,1,128,256]{3,0,2,1:T(2,128)S(1)}, f32[2,1,128,256]{3,0,2,1:T(2,128)S(1)}, u32[]{:S(2)}, u32[]{:S(2)}) %collective-permute-start.1) | collective-permute-done | bytes 262176 | tf_op jit(solution)/shard_map/ppermute | solution.py:19
  24.9 0.0 collective-permute-done.2
  24.9 0.5 pad_maximum_fusion
  25.4 0.0 copy-done.1
  25.4 0.0 copy-start
  25.4 6.0 %bitcast_dynamic-update-slice_fusion.1 = (f32[2,4,128,256]{3,0,2,1:T(2,128)S(1)}, f32[2,128,256]{2,0,1:T(2,128)S(1)}) fusion(f32[2,4,128,256]{3,0,2,1:T(2,128)S(1)} %pad_maximum_fusion, f32[2,1,128,256]{3,0,2,1:T(2,128)S(1)} %collective-permute-done.1, pred[]{:T(512)S(6)} %eq.25, s32[2]{0:T(128)S(1)} %copy-done.1, f32[4,8,128,256]{3,2,1,0:T(8,128)} %bitcast.51), kind=kOutput, calls=%fused_computation.27 | convolution fusion | flops 25231424 | bytes 4981249 | tf_op jit(solution)/shard_map/dot_general | solution.py:60
  31.4 0.7 fusion.31
  32.1 0.3 fusion.29
  32.3 0.3 fusion.30
  32.7 0.0 copy-done
  32.7 1.9 %fusion.15 = f32[2,2,128,256]{3,0,2,1:T(2,128)S(1)} fusion(f32[2,2,128,1]{3,0,2,1:T(2,128)S(1)} %get-tuple-element.191, f32[2,2,128,255]{3,0,2,1:T(2,128)S(1)} %get-tuple-element.193, f32[2,2,128,255]{3,0,2,1:T(2,128)S(1)} %get-tuple-element.192, f32[2,2,128,1]{3,0,2,1:T(2,128)S(1)} %get-tuple-element.190, f32[2,2,1,256]{3,0,2,1:T(2,128)S(1)} %get-tuple-element.187, ...), kind=kLoop, calls=%fused_computation.23 | loop fusion | flops 2228224 | bytes 4718592 | tf_op jit(solution)/shard_map/mul | solution.py:43
  34.7 0.2 fusion.32
  34.8 4.4 %collective-permute-start.3 = (f32[2,1,128,256]{3,0,2,1:T(2,128)S(1)}, f32[2,1,128,256]{3,0,2,1:T(2,128)S(1)}, u32[]{:S(2)}, u32[]{:S(2)}) collective-permute-start(f32[2,1,128,256]{3,0,2,1:T(2,128)S(1)} %get-tuple-element.194), channel_id=1, source_target_pairs={{0,4},{4,8},{8,12},{12,16},{16,20},{20,24},{24,28},{1,5},{5,9},{9,... | collective-permute-start | bytes 786440 | tf_op jit(solution)/shard_map/ppermute | solution.py:19
  39.3 1.5 collective-permute-start.4
  40.7 3.2 %collective-permute-done.3 = f32[2,1,128,256]{3,0,2,1:T(2,128)S(1)} collective-permute-done((f32[2,1,128,256]{3,0,2,1:T(2,128)S(1)}, f32[2,1,128,256]{3,0,2,1:T(2,128)S(1)}, u32[]{:S(2)}, u32[]{:S(2)}) %collective-permute-start.3) | collective-permute-done | bytes 262176 | tf_op jit(solution)/shard_map/ppermute | solution.py:19
  43.9 5.9 %collective-permute-done.4 = f32[2,1,128,256]{3,0,2,1:T(2,128)S(1)} collective-permute-done((f32[2,1,128,256]{3,0,2,1:T(2,128)S(1)}, f32[2,1,128,256]{3,0,2,1:T(2,128)S(1)}, u32[]{:S(2)}, u32[]{:S(2)}) %collective-permute-start.4) | collective-permute-done | bytes 262176 | tf_op jit(solution)/shard_map/ppermute | solution.py:22
  49.8 0.5 pad_maximum_fusion.1
  50.3 0.2 bitcast_dynamic-update-slice_fusion
  50.4 0.7 fusion.27
  51.1 0.3 fusion.25
  51.4 0.3 fusion.26
  51.8 3.2 %fusion.22 = (bf16[2,128,256]{2,1,0:T(8,128)(2,1)}, f32[2,2,128,256]{3,0,2,1:T(2,128)S(1)}) fusion(f32[2,2,128,1]{3,0,2,1:T(2,128)S(1)} %get-tuple-element.183, f32[2,2,128,255]{3,0,2,1:T(2,128)S(1)} %get-tuple-element.185, f32[2,2,128,255]{3,0,2,1:T(2,128)S(1)} %get-tuple-element.184, f32[2,2,128,1]{3,0,2,1:T(2,128)S(1)} %get-tuple-element.182, ...), kind=kLoop, calls=%fused_computation.44 | loop fusion | flops 2293760 | bytes 4849664 | tf_op jit(solution)/shard_map/reduce_sum | solution.py:74
  55.0 0.0 all-reduce.2.cloned.1.call-update
  55.0 35.5 %all-reduce.2.cloned.1.call-done = bf16[2,128,256]{2,1,0:T(8,128)(2,1)} async-done(((bf16[2,128,256]{2,1,0:T(8,128)(2,1)}), bf16[2,128,256]{2,1,0:T(8,128)(2,1)}) %all-reduce.2.cloned.1.call-update) | async-done | bytes 131088 | tf_op jit(solution)/shard_map/psum | solution.py:76
  90.5 0.9 convert_multiply_fusion
  91.4 0.3 subtract_convert_fusion
  91.7 0.9 convolution_bitcast_fusion
  92.5 0.2 copy.52
  92.8 0.1 dynamic_update_slice.13
  92.9 21.1 %while.19 = (s32[]{:T(128)}, f32[2,8]{1,0:T(2,128)S(1)}, bf16[2,65536]{1,0:T(2,128)(2,1)S(1)}, bf16[2,65536]{1,0:T(2,128)(2,1)S(1)}, s32[]{:T(128)}, /*index=5*/...) while((s32[]{:T(128)}, f32[2,8]{1,0:T(2,128)S(1)}, ...), condition=%wide.region_3.4_spmd, body=%wide.region_2.3_spmd.sunk | while | flops 524306 | bytes 2097520 | solution.py:103
  92.9 0.1 collective-permute-start
  93.0 5.8 %collective-permute-done = bf16[2,65536]{1,0:T(2,128)(2,1)S(1)} collective-permute-done((bf16[2,65536]{1,0:T(2,128)(2,1)S(1)}, bf16[2,65536]{1,0:T(2,128)(2,1)S(1)}, u32[]{:S(2)}, u32[]{:S(2)}) %collective-permute-start) | collective-permute-done | bytes 262176 | tf_op jit(solution)/shard_map/while/body/eval_jaxpr/ppermute | solution.py:30
  98.8 0.8 fusion.44
  99.5 0.2 dynamic_update_slice.15
  99.7 0.2 copy.58
  99.9 0.1 collective-permute-start
  100.0 5.8 %collective-permute-done = bf16[2,65536]{1,0:T(2,128)(2,1)S(1)} collective-permute-done((bf16[2,65536]{1,0:T(2,128)(2,1)S(1)}, bf16[2,65536]{1,0:T(2,128)(2,1)S(1)}, u32[]{:S(2)}, u32[]{:S(2)}) %collective-permute-start) | collective-permute-done | bytes 262176 | tf_op jit(solution)/shard_map/while/body/eval_jaxpr/ppermute | solution.py:30
  105.8 0.8 fusion.44
  106.6 0.2 dynamic_update_slice.15
  106.8 0.2 copy.58
  107.0 0.1 collective-permute-start
  107.1 5.8 %collective-permute-done = bf16[2,65536]{1,0:T(2,128)(2,1)S(1)} collective-permute-done((bf16[2,65536]{1,0:T(2,128)(2,1)S(1)}, bf16[2,65536]{1,0:T(2,128)(2,1)S(1)}, u32[]{:S(2)}, u32[]{:S(2)}) %collective-permute-start) | collective-permute-done | bytes 262176 | tf_op jit(solution)/shard_map/while/body/eval_jaxpr/ppermute | solution.py:30
  112.8 0.8 fusion.44
  113.6 0.2 dynamic_update_slice.15
  113.8 0.2 copy.58
  114.0 0.8 copy.32
  114.9 21.3 %psum.15 = f32[2,8]{1,0:T(2,128)S(1)} all-reduce(f32[2,8]{1,0:T(2,128)S(1)} %broadcast_multiply_fusion), channel_id=1, replica_groups=mesh['space'=8,'member'=4] {'space'}, use_global_device_ids=true, to_apply=%region_4.5 | all-reduce | flops 16 | bytes 128 | tf_op jit(solution)/shard_map/psum | solution.py:105
  136.2 5.1 %all-gather = f32[4,2,8]{2,1,0:T(2,128)S(1)} all-gather(f32[1,2,8]{2,1,0:T(2,128)S(1)} %bitcast.55), channel_id=1, replica_groups=mesh['space'=8,'member'=4] {'member'}, dimensions={0}, use_global_device_ids=true | all-gather | bytes 320 | tf_op jit(solution)/shard_map/all_gather | solution.py:106
  141.3 0.1 copy.28
  141.3 0.1 copy.29
  141.4 0.7 cholesky.19
  142.1 0.1 copy.30
  142.2 0.1 select_reduce_fusion
  142.3 0.7 compare_reduce_fusion
  143.1 1.3 select_bitcast_fusion
  (6 shorter events, 0.0 us)
Async XLA Ops:
  7.2 18.2 %copy-start.1 = (s32[2]{0:T(128)S(1)}, s32[2]{0:T(128)}, u32[]{:S(2)}) copy-start(s32[2]{0:T(128)} %param.15) | copy-start | bytes 28
  7.2 83.3 %all-reduce.2.cloned.1.call-start = ((), (), s32[]{:S(2)}) async-start(), calls=%async_computation | async-start | bytes 262144 | tf_op jit(solution)/shard_map/psum | solution.py:76
  8.9 16.0 %collective-permute-start.1 = (f32[2,1,128,256]{3,0,2,1:T(2,128)S(1)}, f32[2,1,128,256]{3,0,2,1:T(2,128)S(1)}, u32[]{:S(2)}, u32[]{:S(2)}) collective-permute-start(f32[2,1,128,256]{3,0,2,1:T(2,128)S(1)} %get-tuple-element.196), channel_id=1, source_target_pairs={{0,4},{4,8},{8,12},{12,16},{16,20},{20,24},{24,28},{1,5},{5,9},{9,... | collective-permute-start | bytes 786440 | tf_op jit(solution)/shard_map/ppermute | solution.py:19
  13.7 11.2 %collective-permute-start.2 = (f32[2,1,128,256]{3,0,2,1:T(2,128)S(1)}, f32[2,1,128,256]{3,0,2,1:T(2,128)S(1)}, u32[]{:S(2)}, u32[]{:S(2)}) collective-permute-start(f32[2,1,128,256]{3,0,2,1:T(2,128)S(1)} %get-tuple-element.197), channel_id=1, source_target_pairs={{4,0},{8,4},{12,8},{16,12},{20,16},{24,20},{28,24},{5,1},{9,5},{13... | collective-permute-start | bytes 786440 | tf_op jit(solution)/shard_map/ppermute | solution.py:22
  25.4 7.3 %copy-start = (f32[2,128,256]{2,1,0:T(8,128)S(1)}, f32[2,128,256]{2,1,0:T(8,128)}, u32[]{:S(2)}) copy-start(f32[2,128,256]{2,1,0:T(8,128)} %param.12) | copy-start | bytes 786436
  34.8 9.1 %collective-permute-start.3 = (f32[2,1,128,256]{3,0,2,1:T(2,128)S(1)}, f32[2,1,128,256]{3,0,2,1:T(2,128)S(1)}, u32[]{:S(2)}, u32[]{:S(2)}) collective-permute-start(f32[2,1,128,256]{3,0,2,1:T(2,128)S(1)} %get-tuple-element.194), channel_id=1, source_target_pairs={{0,4},{4,8},{8,12},{12,16},{16,20},{20,24},{24,28},{1,5},{5,9},{9,... | collective-permute-start | bytes 786440 | tf_op jit(solution)/shard_map/ppermute | solution.py:19
  39.3 10.5 %collective-permute-start.4 = (f32[2,1,128,256]{3,0,2,1:T(2,128)S(1)}, f32[2,1,128,256]{3,0,2,1:T(2,128)S(1)}, u32[]{:S(2)}, u32[]{:S(2)}) collective-permute-start(f32[2,1,128,256]{3,0,2,1:T(2,128)S(1)} %get-tuple-element.195), channel_id=1, source_target_pairs={{4,0},{8,4},{12,8},{16,12},{20,16},{24,20},{28,24},{5,1},{9,5},{13... | collective-permute-start | bytes 786440 | tf_op jit(solution)/shard_map/ppermute | solution.py:22
  92.9 5.8 %collective-permute-start = (bf16[2,65536]{1,0:T(2,128)(2,1)S(1)}, bf16[2,65536]{1,0:T(2,128)(2,1)S(1)}, u32[]{:S(2)}, u32[]{:S(2)}) collective-permute-start(bf16[2,65536]{1,0:T(2,128)(2,1)S(1)} %get-tuple-element.244), channel_id=1, source_target_pairs={{3,0},{0,1},{1,2},{2,3},{7,4},{4,5},{5,6},{6,7},{11,8},{8,9},{9,10... | collective-permute-start | bytes 786440 | tf_op jit(solution)/shard_map/while/body/eval_jaxpr/ppermute | solution.py:30
  99.9 5.8 %collective-permute-start = (bf16[2,65536]{1,0:T(2,128)(2,1)S(1)}, bf16[2,65536]{1,0:T(2,128)(2,1)S(1)}, u32[]{:S(2)}, u32[]{:S(2)}) collective-permute-start(bf16[2,65536]{1,0:T(2,128)(2,1)S(1)} %get-tuple-element.244), channel_id=1, source_target_pairs={{3,0},{0,1},{1,2},{2,3},{7,4},{4,5},{5,6},{6,7},{11,8},{8,9},{9,10... | collective-permute-start | bytes 786440 | tf_op jit(solution)/shard_map/while/body/eval_jaxpr/ppermute | solution.py:30
  107.0 5.8 %collective-permute-start = (bf16[2,65536]{1,0:T(2,128)(2,1)S(1)}, bf16[2,65536]{1,0:T(2,128)(2,1)S(1)}, u32[]{:S(2)}, u32[]{:S(2)}) collective-permute-start(bf16[2,65536]{1,0:T(2,128)(2,1)S(1)} %get-tuple-element.244), channel_id=1, source_target_pairs={{3,0},{0,1},{1,2},{2,3},{7,4},{4,5},{5,6},{6,7},{11,8},{8,9},{9,10... | collective-permute-start | bytes 786440 | tf_op jit(solution)/shard_map/while/body/eval_jaxpr/ppermute | solution.py:30
Sparse Core Ops, SparseCore 0:
  55.1 35.3 all-reduce.1
where the time goes:
time: 151 us
  waiting for transfers between devices  70.7 us (47%)
  blocking collectives  26.4 us (17%)
  between operations  14.3 us (9%)
  starting transfers between devices  12.2 us (8%)
  other arithmetic  11.2 us (7%)
  matrix products  9.16 us (6%)
  local copies, waits for them, and re-layouts  7.04 us (5%)
    psum x1, waiting for transfers between devices, local(): lax.psum(member_sum.astype(jnp.bfloat16), 'member').astype(jnp.float32)  35.5 us
    psum x1, blocking collectives, local(): summed = lax.psum(gram_tile, 'space')  21.3 us
    ppermute x3, waiting for transfers between devices, from_behind(): return lax.ppermute(block, axis, route)  17.3 us
    ppermute x2, waiting for transfers between devices, extended_2(): lax.ppermute(lax.slice_in_dim(block, block.shape[dim] - width, None, axis...  12 us
    ppermute x2, starting transfers between devices, extended_2(): lax.ppermute(lax.slice_in_dim(block, block.shape[dim] - width, None, axis...  9.26 us
    dot_general x1, matrix products, local(): jnp.dot(pattern_pick, inflow_table.reshape(patterns, plane_rows * plane_c...  5.97 us
    ppermute x2, waiting for transfers between devices, extended_2(): lax.ppermute(lax.slice_in_dim(block, 0, width, axis=dim), axis, backward)  5.88 us
    all_gather x1, blocking collectives, local(): gram_full = lax.all_gather(summed, 'member', axis=0, tiled=True)  5.06 us
  transfers between devices with their start and end apart: 8, of which 7 were waited for; matrix products, arithmetic and copies ran while one was open for 1% of the time, Pallas kernels for 0%

commit v1 on v0

v1 whole, which is shorter than its diff:
```python
import functools

import jax
import jax.numpy as jnp
from jax import lax
from jax.experimental import pallas as pl
from jax.experimental.pallas import tpu as pltpu
from jax.sharding import PartitionSpec as P

STEPS = 2

kappa_rate = 0.05
shrink_weight = 0.1
MESH = pl.DeviceIdType.MESH
HIGHEST = lax.Precision.HIGHEST


def kernel(
    slabs, groups, index, fields, velocity, building, table, out_f, out_r,
    f_v, v_v, b_v, t_v, coef_a, coef_b, coef_c, u1, u2, w_in, e_in, e_out,
    part_out, part_in, pair_rows, gram_a, gram_b,
    load_sem, save_sem, up_send, up_recv, down_send, down_recv,
    part_send, part_recv, a_send, a_recv, b_send, b_recv,
):
    mem, depth, rows, cols = f_v.shape
    members = mem * groups
    part_rows = part_out.shape[2]
    per_plane = groups // depth
    space = lax.axis_index("space")
    group = lax.axis_index("member")
    first = space == 0
    last = space == slabs - 1

    loads = [
        pltpu.make_async_copy(fields, f_v, load_sem.at[0]),
        pltpu.make_async_copy(velocity, v_v, load_sem.at[1]),
        pltpu.make_async_copy(building, b_v, load_sem.at[2]),
    ]
    for load in loads:
        load.start()
    table_load = pltpu.make_async_copy(table, t_v, load_sem.at[3])

    @pl.when(first)
    def _():
        table_load.start()

    barrier = pltpu.get_barrier_semaphore()
    for o in range(1, slabs):
        pl.semaphore_signal(
            barrier, inc=1, device_id=(lax.rem(space + o, slabs), group), device_id_type=MESH
        )
    for o in range(1, groups):
        pl.semaphore_signal(
            barrier, inc=1, device_id=(space, lax.rem(group + o, groups)), device_id_type=MESH
        )

    def up(step, m):
        source = fields if step == 0 else u1
        return pltpu.make_async_remote_copy(
            src_ref=source.at[m, depth - 1], dst_ref=w_in.at[step, m],
            send_sem=up_send.at[step, m], recv_sem=up_recv.at[step, m],
            device_id=(lax.rem(space + 1, slabs), group), device_id_type=MESH,
        )

    def down(step, m):
        return pltpu.make_async_remote_copy(
            src_ref=e_out.at[step, m], dst_ref=e_in.at[step, m],
            send_sem=down_send.at[step, m], recv_sem=down_recv.at[step, m],
            device_id=(lax.rem(space + slabs - 1, slabs), group), device_id_type=MESH,
        )

    loads[0].wait()
    for m in range(mem):
        e_out[0, m] = f_v[m, 0].astype(e_out.dtype)
    pl.semaphore_wait(barrier, slabs + groups - 2)

    @pl.when(jnp.logical_not(last))
    def _():
        for m in range(mem):
            up(0, m).start()

    @pl.when(jnp.logical_not(first))
    def _():
        for m in range(mem):
            down(0, m).start()

    @pl.when(last)
    def _():
        e_in[...] = jnp.zeros_like(e_in)

    loads[1].wait()
    loads[2].wait()
    for d in range(depth):
        fluid = (1 - b_v[d]).astype(jnp.float32)
        v = v_v[d]
        coef_a[d] = fluid * ((1.0 - 6.0 * kappa_rate) - v)
        coef_b[d] = fluid * (v + kappa_rate)
        coef_c[d] = fluid * kappa_rate

    @pl.when(first)
    def _():
        table_load.wait()
        for m in range(mem):
            plane = t_v[index[m]]
            for step in range(STEPS):
                w_in[step, m] = plane

    def part_copy(o):
        target = lax.rem(group + o, groups)
        return pltpu.make_async_remote_copy(
            src_ref=part_out.at[target], dst_ref=part_in.at[group],
            send_sem=part_send.at[o], recv_sem=part_recv.at[o],
            device_id=(space, target), device_id_type=MESH,
        )

    def finish(m, d):
        value = u2[m, d]
        pltpu.make_async_copy(u2.at[m, d], out_f.at[m, d], save_sem.at[m, d]).start()
        for i in range(per_plane):
            part_out[d * per_plane + i, m] = value[i * part_rows:(i + 1) * part_rows].astype(part_out.dtype)
        if m == mem - 1:
            for o in range(1, groups):
                @pl.when(lax.rem(group + o, groups) // per_plane == d)
                def _():
                    part_copy(o).start()

    old = f_v
    for step in range(STEPS):
        new = u1 if step == 0 else u2
        for m in range(mem):
            for d in range(depth):
                c = old[m, d]
                s = (
                    pltpu.roll(c, 1, 0) + pltpu.roll(c, rows - 1, 0)
                    + pltpu.roll(c, 1, 1) + pltpu.roll(c, cols - 1, 1)
                )
                if d < depth - 1:
                    s = s + old[m, d + 1]
                p = coef_a[d] * c + coef_c[d] * s
                if d > 0:
                    p = p + coef_b[d] * old[m, d - 1]
                new[m, d] = p
        for m in range(mem):
            @pl.when(jnp.logical_not(last))
            def _():
                down(step, m).wait_recv()

            new[m, depth - 1] += coef_c[depth - 1] * e_in[step, m].astype(jnp.float32)
            if step < STEPS - 1:
                @pl.when(jnp.logical_not(last))
                def _():
                    up(step + 1, m).start()
            else:
                finish(m, depth - 1)
        for m in range(mem):
            @pl.when(jnp.logical_not(first))
            def _():
                up(step, m).wait_recv()

            new[m, 0] += coef_b[0] * w_in[step, m]
            if step < STEPS - 1:
                e_out[step + 1, m] = new[m, 0].astype(e_out.dtype)

                @pl.when(jnp.logical_not(first))
                def _():
                    down(step + 1, m).start()
            else:
                finish(m, 0)
        old = new
    for d in range(1, depth - 1):
        for m in range(mem):
            finish(m, d)

    part_in[group] = part_out[group]
    for o in range(1, groups):
        part_copy(o).wait_recv()

    sums = {}
    for r in range(part_rows // 16):
        for l in range(cols // 128):
            us = [
                part_in[i // mem, i % mem, r * 16:(r + 1) * 16, l * 128:(l + 1) * 128].astype(jnp.float32)
                for i in range(members)
            ]
            mean = functools.reduce(lambda a, b: a + b, us) / members
            an = [(u - mean).astype(jnp.bfloat16).astype(jnp.float32) for u in us]
            for i in range(members):
                for j in range(i, members):
                    q = an[i] * an[j]
                    q = q[:8] + q[8:]
                    sums[i, j] = sums[i, j] + q if (i, j) in sums else q
    padded = pair_rows.shape[0]
    if padded > members * members:
        pair_rows[members * members:] = jnp.zeros((padded - members * members, 128), jnp.float32)
    for (i, j), q in sums.items():
        q = jnp.sum(q, 0, keepdims=True)
        pair_rows[i * members + j:i * members + j + 1] = q
        if i != j:
            pair_rows[j * members + i:j * members + i + 1] = q
    packed = lax.dot_general(
        jnp.ones((8, 128), jnp.float32), pair_rows[...], (((1,), (1,)), ((), ())),
        precision=HIGHEST, preferred_element_type=jnp.float32,
    )[0:1]

    def copy_a(o):
        return pltpu.make_async_remote_copy(
            src_ref=gram_a.at[group], dst_ref=gram_a.at[group],
            send_sem=a_send.at[o], recv_sem=a_recv.at[o],
            device_id=(space, lax.rem(group + o, groups)), device_id_type=MESH,
        )

    def copy_b(o):
        return pltpu.make_async_remote_copy(
            src_ref=gram_b.at[space], dst_ref=gram_b.at[space],
            send_sem=b_send.at[o], recv_sem=b_recv.at[o],
            device_id=(lax.rem(space + o, slabs), group), device_id_type=MESH,
        )

    gram_a[group] = packed
    for o in range(1, groups):
        copy_a(o).start()
    for o in range(1, groups):
        copy_a(o).wait_recv()
    gram_b[space] = jnp.sum(gram_a[...], 0)
    for o in range(1, slabs):
        copy_b(o).start()
    for o in range(1, slabs):
        copy_b(o).wait_recv()
    total = jnp.sum(gram_b[...], 0) / (slabs * depth * rows * cols)

    lane = lax.broadcasted_iota(jnp.int32, (members, padded), 1)
    row = lax.broadcasted_iota(jnp.int32, (members, padded), 0)
    spread = jnp.where(
        (lane >= row * members) & (lane < (row + 1) * members),
        jnp.broadcast_to(total, (members, padded)), 0.0,
    )
    source = lax.broadcasted_iota(jnp.int32, (padded, 128), 0)
    target = lax.broadcasted_iota(jnp.int32, (padded, 128), 1)
    fold = jnp.where(lax.rem(source, members) == target, 1.0, 0.0)
    gram = lax.dot_general(
        spread, fold, (((1,), (0,)), ((), ())), precision=HIGHEST, preferred_element_type=jnp.float32
    )
    row = lax.broadcasted_iota(jnp.int32, (members, 128), 0)
    lane = lax.broadcasted_iota(jnp.int32, (members, 128), 1)
    left = gram + jnp.where(row == lane, shrink_weight, 0.0)
    factor = jnp.zeros_like(left)
    for k in range(members):
        pivot = left[k:k + 1, k:k + 1]
        inverse = lax.rsqrt(pivot)
        inverse = inverse * (1.5 - 0.5 * pivot * inverse * inverse)
        line = left[k:k + 1] * inverse
        factor = jnp.where((row == k) & (lane >= k), line, factor)
        if k < members - 1:
            left = left - (left[:, k:k + 1] * inverse) * line
    out_r[...] = factor[:, :members]

    for m in range(mem):
        for d in range(depth):
            pltpu.make_async_copy(u2.at[m, d], out_f.at[m, d], save_sem.at[m, d]).wait()

    @pl.when(jnp.logical_not(last))
    def _():
        for step in range(STEPS):
            for m in range(mem):
                up(step, m).wait_send()

    @pl.when(jnp.logical_not(first))
    def _():
        for step in range(STEPS):
            for m in range(mem):
                down(step, m).wait_send()

    for o in range(1, groups):
        part_copy(o).wait_send()
        copy_a(o).wait_send()
    for o in range(1, slabs):
        copy_b(o).wait_send()


def local(slabs, groups, fields, velocity, building, inflow_table, inflow_index):
    mem, depth, rows, cols = fields.shape
    members = mem * groups
    padded = -(-members * members // 128) * 128
    f32, low = jnp.float32, jnp.bfloat16
    hbm = pl.BlockSpec(memory_space=pl.ANY)
    vmem, dma = pltpu.VMEM, pltpu.SemaphoreType.DMA
    slab = (depth, rows, cols)
    part = (groups, mem, depth * rows // groups, cols)
    return pl.pallas_call(
        functools.partial(kernel, slabs, groups),
        out_shape=(
            jax.ShapeDtypeStruct(fields.shape, f32),
            jax.ShapeDtypeStruct((members, members), f32),
        ),
        in_specs=[pl.BlockSpec(memory_space=pltpu.SMEM), hbm, hbm, hbm, hbm],
        out_specs=(hbm, pl.BlockSpec(memory_space=pltpu.VMEM)),
        scratch_shapes=[
            vmem(fields.shape, f32), vmem(slab, f32), vmem(slab, jnp.int32), vmem(inflow_table.shape, f32),
            vmem(slab, f32), vmem(slab, f32), vmem(slab, f32),
            vmem(fields.shape, f32), vmem(fields.shape, f32),
            vmem((STEPS, mem, rows, cols), f32),
            vmem((STEPS, mem, rows, cols), low), vmem((STEPS, mem, rows, cols), low),
            vmem(part, low), vmem(part, low), vmem((padded, 128), f32),
            vmem((groups, 1, padded), f32), vmem((slabs, 1, padded), f32),
            dma((4,)), dma((mem, depth)),
            dma((STEPS, mem)), dma((STEPS, mem)), dma((STEPS, mem)), dma((STEPS, mem)),
            dma((groups,)), dma((groups,)), dma((groups,)), dma((groups,)),
            dma((slabs,)), dma((slabs,)),
        ],
        compiler_params=pltpu.CompilerParams(
            collective_id=0, has_side_effects=True, vmem_limit_bytes=48 * 1024 * 1024
        ),
    )(inflow_index, fields, velocity, building, inflow_table)


def solution(mesh):
    placed = (
        P("member", "space", None, None),
        P("space", None, None),
        P("space", None, None),
        P(),
        P("member"),
    )
    return jax.shard_map(
        functools.partial(local, mesh.shape["space"], mesh.shape["member"]),
        mesh=mesh,
        in_specs=placed,
        out_specs=(P("member", "space", None, None), P()),
        check_vma=False,
    )
```

time: 151 us -> 47.7 us (0.32)
  waiting for transfers between devices: 70.7 us -> 0 us
  Pallas kernels: 0 us -> 39.6 us
  blocking collectives: 26.4 us -> 0 us
  between operations: 14.3 us -> 0.65 us
  starting transfers between devices: 12.2 us -> 0 us
  other arithmetic: 11.2 us -> 0 us
  matrix products: 9.16 us -> 0 us
    pallas_call x0 -> x1, Pallas kernels: none -> 39.6 us  [local(): pl.pallas_call(functools.partial(kernel, slabs, groups), out_shape=(jax.S...]
    psum x1 -> x0, waiting for transfers between devices: 35.5 us -> none  [local(): lax.psum(member_sum.astype(jnp.bfloat16), 'member').astype(jnp.float32)]
    ppermute x7 -> x0, waiting for transfers between devices: 35.2 us -> none  [the longest x3 17.3 us: from_behind(): return lax.ppermute(block, axis, route)]
    psum x1 -> x0, blocking collectives: 21.3 us -> none  [local(): summed = lax.psum(gram_tile, 'space')]
    ppermute x7 -> x0, starting transfers between devices: 12.2 us -> none  [the longest x2 9.26 us: extended_2(): lax.ppermute(lax.slice_in_dim(block, block.shape[dim] - width, None, axis...]
    dot_general x5 -> x0, matrix products: 9.16 us -> none  [the longest x1 5.97 us: local(): jnp.dot(pattern_pick, inflow_table.reshape(patterns, plane_rows * plane_c...]
    all_gather x1 -> x0, blocking collectives: 5.06 us -> none  [local(): gram_full = lax.all_gather(summed, 'member', axis=0, tiled=True)]
    unnamed x8 -> x12, local copies, waits for them, and re-layouts: 2.56 us -> 7.16 us
  transfers between devices with their start and end apart: 8 -> 0, of which waited for: 7 -> 0; matrix products, arithmetic and copies ran while one was open for 1% -> 0% of each run, Pallas kernels for 0% -> 0%
where the time goes in v1:
time: 47.7 us; the launch traced here: 47.4 us
  Pallas kernels  39.6 us (83%)
  local copies, waits for them, and re-layouts  7.16 us (15%)
  between operations  0.65 us (1%)
    pallas_call x1, Pallas kernels, local(): pl.pallas_call(functools.partial(kernel, slabs, groups), out_shape=(jax.S...  39.6 us
    unnamed x12, local copies, waits for them, and re-layouts  7.16 us

profile of v1, /device:TPU:0, one launch (start us, length us, event | category | flops | bytes accessed | tf_op | source)
XLA Modules:
  0.0 47.4 jit_solution(8956617196031024810)
XLA Ops:
  0.6 0.0 copy-start
  0.6 2.2 %copy-done = f32[32,128,256]{2,1,0:T(8,128)S(1)} copy-done((f32[32,128,256]{2,1,0:T(8,128)S(1)}, f32[32,128,256]{2,1,0:T(8,128)}, u32[]{:S(2)}) %copy-start) | copy-done | bytes 4194328
  2.8 0.0 copy-start.1
  2.8 1.0 %copy-done.1 = f32[2,2,128,256]{3,2,1,0:T(8,128)S(1)} copy-done((f32[2,2,128,256]{3,2,1,0:T(8,128)S(1)}, f32[2,2,128,256]{3,2,1,0:T(8,128)}, u32[]{:S(2)}) %copy-start.1) | copy-done | bytes 524312
  3.9 0.0 copy-start.2
  3.9 0.9 %copy-done.2 = f32[2,128,256]{2,1,0:T(8,128)S(1)} copy-done((f32[2,128,256]{2,1,0:T(8,128)S(1)}, f32[2,128,256]{2,1,0:T(8,128)}, u32[]{:S(2)}) %copy-start.2) | copy-done | bytes 262168
  4.8 0.0 copy-start.3
  4.8 0.9 %copy-done.3 = s32[2,128,256]{2,1,0:T(8,128)S(1)} copy-done((s32[2,128,256]{2,1,0:T(8,128)S(1)}, s32[2,128,256]{2,1,0:T(8,128)}, u32[]{:S(2)}) %copy-start.3) | copy-done | bytes 262168
  5.8 0.0 copy-start.4
  5.8 0.7 %copy-done.4 = s32[2]{0:T(128)S(1)} copy-done((s32[2]{0:T(128)S(1)}, s32[2]{0:T(128)}, u32[]{:S(2)}) %copy-start.4) | copy-done | bytes 32
  6.4 39.6 %shard_map.68 = (f32[2,2,128,256]{3,2,1,0:T(8,128)S(1)}, f32[8,8]{1,0:T(8,128)S(1)}) custom-call(s32[2]{0:T(128)S(1)} %copy-done.4, f32[2,2,128,256]{3,2,1,0:T(8,128)S(1)} %copy-done.1, f32[2,128,256]{2,1,0:T(8,128)S(1)} %copy-done.2, s32[2,128,256]{2,1,0:T(8,128)S(1)} %copy-done.3, f32[32,128,256]{2,1,0:T(8,128)S(1)} %copy-done), custom_call_target="tpu_custom_call" | custom-call | tf_op jit(solution)/shard_map/pallas_call | solution.py:289
  46.0 0.8 %copy.9 = f32[2,2,128,256]{3,2,1,0:T(8,128)} copy(f32[2,2,128,256]{3,2,1,0:T(8,128)S(1)} %get-tuple-element.4) | data formatting | bytes 1048576
  46.8 0.6 %copy.10 = f32[8,8]{1,0:T(8,128)} copy(f32[8,8]{1,0:T(8,128)S(1)} %get-tuple-element.5) | data formatting | bytes 512
Async XLA Ops:
  0.6 2.2 %copy-start = (f32[32,128,256]{2,1,0:T(8,128)S(1)}, f32[32,128,256]{2,1,0:T(8,128)}, u32[]{:S(2)}) copy-start(f32[32,128,256]{2,1,0:T(8,128)} %table.1) | copy-start | bytes 12582916
  2.8 1.0 %copy-start.1 = (f32[2,2,128,256]{3,2,1,0:T(8,128)S(1)}, f32[2,2,128,256]{3,2,1,0:T(8,128)}, u32[]{:S(2)}) copy-start(f32[2,2,128,256]{3,2,1,0:T(8,128)} %fields.1) | copy-start | bytes 1572868
  3.9 0.9 %copy-start.2 = (f32[2,128,256]{2,1,0:T(8,128)S(1)}, f32[2,128,256]{2,1,0:T(8,128)}, u32[]{:S(2)}) copy-start(f32[2,128,256]{2,1,0:T(8,128)} %velocity.1) | copy-start | bytes 786436
  4.8 0.9 %copy-start.3 = (s32[2,128,256]{2,1,0:T(8,128)S(1)}, s32[2,128,256]{2,1,0:T(8,128)}, u32[]{:S(2)}) copy-start(s32[2,128,256]{2,1,0:T(8,128)} %building.1) | copy-start | bytes 786436
  5.8 0.7 %copy-start.4 = (s32[2]{0:T(128)S(1)}, s32[2]{0:T(128)}, u32[]{:S(2)}) copy-start(s32[2]{0:T(128)} %index.1) | copy-start | bytes 28

commit v2 on v1

--- a/solution.py
+++ b/solution.py
@@ -11,15 +11,16 @@
 
 kappa_rate = 0.05
 shrink_weight = 0.1
+LEVELS = 32767.0
 MESH = pl.DeviceIdType.MESH
 HIGHEST = lax.Precision.HIGHEST
 
 
 def kernel(
     slabs, groups, index, fields, velocity, building, table, out_f, out_r,
-    f_v, v_v, b_v, t_v, coef_a, coef_b, coef_c, u1, u2, w_in, e_in, e_out,
+    f_v, v_v, b_v, t_v, coef_a, coef_b, coef_c, u1, u2, inflow, w_in, w_out, scale_in, scale_out, e_in, e_out,
     part_out, part_in, pair_rows, gram_a, gram_b,
-    load_sem, save_sem, up_send, up_recv, down_send, down_recv,
+    load_sem, save_sem, up_send, up_recv, scale_send, scale_recv, down_send, down_recv,
     part_send, part_recv, a_send, a_recv, b_send, b_recv,
 ):
     mem, depth, rows, cols = f_v.shape
@@ -55,12 +56,24 @@
         )
 
     def up(step, m):
-        source = fields if step == 0 else u1
-        return pltpu.make_async_remote_copy(
-            src_ref=source.at[m, depth - 1], dst_ref=w_in.at[step, m],
-            send_sem=up_send.at[step, m], recv_sem=up_recv.at[step, m],
-            device_id=(lax.rem(space + 1, slabs), group), device_id_type=MESH,
-        )
+        target = (lax.rem(space + 1, slabs), group)
+        return (
+            pltpu.make_async_remote_copy(
+                src_ref=scale_out.at[step, m], dst_ref=scale_in.at[step, m],
+                send_sem=scale_send.at[step, m], recv_sem=scale_recv.at[step, m],
+                device_id=target, device_id_type=MESH,
+            ),
+            pltpu.make_async_remote_copy(
+                src_ref=w_out.at[step, m], dst_ref=w_in.at[step, m],
+                send_sem=up_send.at[step, m], recv_sem=up_recv.at[step, m],
+                device_id=target, device_id_type=MESH,
+            ),
+        )
+
+    def encode(step, m, plane):
+        top = jnp.maximum(jnp.max(jnp.abs(plane), 0, keepdims=True), 1e-30)
+        scale_out[step, m] = top * (1.0 / LEVELS)
+        w_out[step, m] = jnp.round(plane * (LEVELS / top)).astype(jnp.int32).astype(jnp.int16)
 
     def down(step, m):
         return pltpu.make_async_remote_copy(
@@ -71,13 +84,15 @@
 
     loads[0].wait()
     for m in range(mem):
+        encode(0, m, f_v[m, depth - 1])
         e_out[0, m] = f_v[m, 0].astype(e_out.dtype)
     pl.semaphore_wait(barrier, slabs + groups - 2)
 
     @pl.when(jnp.logical_not(last))
     def _():
         for m in range(mem):
-            up(0, m).start()
+            for copy in up(0, m):
+                copy.start()
 
     @pl.when(jnp.logical_not(first))
     def _():
@@ -101,9 +116,7 @@
     def _():
         table_load.wait()
         for m in range(mem):
-            plane = t_v[index[m]]
-            for step in range(STEPS):
-                w_in[step, m] = plane
+            inflow[m] = t_v[index[m]]
 
     def part_copy(o):
         target = lax.rem(group + o, groups)
@@ -147,17 +160,22 @@
 
             new[m, depth - 1] += coef_c[depth - 1] * e_in[step, m].astype(jnp.float32)
             if step < STEPS - 1:
+                encode(step + 1, m, new[m, depth - 1])
+
                 @pl.when(jnp.logical_not(last))
                 def _():
-                    up(step + 1, m).start()
+                    for copy in up(step + 1, m):
+                        copy.start()
             else:
                 finish(m, depth - 1)
         for m in range(mem):
             @pl.when(jnp.logical_not(first))
             def _():
-                up(step, m).wait_recv()
-
-            new[m, 0] += coef_b[0] * w_in[step, m]
+                for copy in up(step, m):
+                    copy.wait_recv()
+                inflow[m] = w_in[step, m].astype(jnp.int32).astype(jnp.float32) * scale_in[step, m]
+
+            new[m, 0] += coef_b[0] * inflow[m]
             if step < STEPS - 1:
                 e_out[step + 1, m] = new[m, 0].astype(e_out.dtype)
 
@@ -262,7 +280,8 @@
     def _():
         for step in range(STEPS):
             for m in range(mem):
-                up(step, m).wait_send()
+                for copy in up(step, m):
+                    copy.wait_send()
 
     @pl.when(jnp.logical_not(first))
     def _():
@@ -282,7 +301,7 @@
     members = mem * groups
     padded = -(-members * members // 128) * 128
     f32, low = jnp.float32, jnp.bfloat16
-    hbm = pl.BlockSpec(memory_space=pl.ANY)
+    hbm = pl.BlockSpec(memory_space=pltpu.HBM)
     vmem, dma = pltpu.VMEM, pltpu.SemaphoreType.DMA
     slab = (depth, rows, cols)
     part = (groups, mem, depth * rows // groups, cols)
@@ -298,17 +317,20 @@
             vmem(fields.shape, f32), vmem(slab, f32), vmem(slab, jnp.int32), vmem(inflow_table.shape, f32),
             vmem(slab, f32), vmem(slab, f32), vmem(slab, f32),
             vmem(fields.shape, f32), vmem(fields.shape, f32),
-            vmem((STEPS, mem, rows, cols), f32),
+            vmem((mem, rows, cols), f32),
+            vmem((STEPS, mem, rows, cols), jnp.int16), vmem((STEPS, mem, rows, cols), jnp.int16),
+            vmem((STEPS, mem, 1, cols), f32), vmem((STEPS, mem, 1, cols), f32),
             vmem((STEPS, mem, rows, cols), low), vmem((STEPS, mem, rows, cols), low),
             vmem(part, low), vmem(part, low), vmem((padded, 128), f32),
             vmem((groups, 1, padded), f32), vmem((slabs, 1, padded), f32),
             dma((4,)), dma((mem, depth)),
             dma((STEPS, mem)), dma((STEPS, mem)), dma((STEPS, mem)), dma((STEPS, mem)),
+            dma((STEPS, mem)), dma((STEPS, mem)),
             dma((groups,)), dma((groups,)), dma((groups,)), dma((groups,)),
             dma((slabs,)), dma((slabs,)),
         ],
         compiler_params=pltpu.CompilerParams(
-            collective_id=0, has_side_effects=True, vmem_limit_bytes=48 * 1024 * 1024
+            collective_id=0, has_side_effects=True, vmem_limit_bytes=64 * 1024 * 1024
         ),
     )(inflow_index, fields, velocity, building, inflow_table)
 

time: 47.7 us -> 37.7 us (0.79)
  Pallas kernels: 39.6 us -> 33.7 us
  local copies, waits for them, and re-layouts: 7.16 us -> 3.13 us
    pallas_call x1, Pallas kernels: 39.6 us -> 33.7 us  [local(): pl.pallas_call(functools.partial(kernel, slabs, groups), out_shape=(jax.S...]
    unnamed x12 -> x2, local copies, waits for them, and re-layouts: 7.16 us -> 3.13 us
where the time goes in v2:
time: 37.7 us; the launch traced here: 37.5 us
  Pallas kernels  33.7 us (89%)
  local copies, waits for them, and re-layouts  3.13 us (8%)
  between operations  0.64 us (2%)
    pallas_call x1, Pallas kernels, local(): pl.pallas_call(functools.partial(kernel, slabs, groups), out_shape=(jax.S...  33.7 us
    unnamed x2, local copies, waits for them, and re-layouts  3.13 us

profile of v2, /device:TPU:0, one launch (start us, length us, event | category | flops | bytes accessed | tf_op | source)
XLA Modules:
  0.0 37.5 jit_solution(1133106508890282748)
XLA Ops:
  0.6 33.7 %shard_map.68 = (f32[2,2,128,256]{3,2,1,0:T(8,128)}, f32[8,8]{1,0:T(8,128)}) custom-call(s32[2]{0:T(128)} %index.1, f32[2,2,128,256]{3,2,1,0:T(8,128)} %fields.1, f32[2,128,256]{2,1,0:T(8,128)} %velocity.1, s32[2,128,256]{2,1,0:T(8,128)} %building.1, f32[32,128,256]{2,1,0:T(8,128)} %table.1), custom_call_target="tpu_custom_call" | custom-call | tf_op jit(solution)/shard_map/pallas_call | solution.py:308
  34.4 1.9 %copy.9 = f32[2,2,128,256]{3,2,1,0:T(8,128)} copy(f32[2,2,128,256]{3,2,1,0:T(8,128)} %get-tuple-element.4) | data formatting | bytes 1048576
  36.2 1.3 %copy.10 = f32[8,8]{1,0:T(8,128)} copy(f32[8,8]{1,0:T(8,128)} %get-tuple-element.5) | data formatting | bytes 512

commit v3 on v2

--- a/solution.py
+++ b/solution.py
@@ -19,9 +19,9 @@
 def kernel(
     slabs, groups, index, fields, velocity, building, table, out_f, out_r,
     f_v, v_v, b_v, t_v, coef_a, coef_b, coef_c, u1, u2, inflow, w_in, w_out, scale_in, scale_out, e_in, e_out,
-    part_out, part_in, pair_rows, gram_a, gram_b,
+    part_out, part_in, pair_rows, gram_b,
     load_sem, save_sem, up_send, up_recv, scale_send, scale_recv, down_send, down_recv,
-    part_send, part_recv, a_send, a_recv, b_send, b_recv,
+    part_send, part_recv, b_send, b_recv,
 ):
     mem, depth, rows, cols = f_v.shape
     members = mem * groups
@@ -32,6 +32,9 @@
     first = space == 0
     last = space == slabs - 1
 
+    def partner(o):
+        return lax.rem(space + o // groups, slabs), lax.rem(group + o % groups, groups)
+
     loads = [
         pltpu.make_async_copy(fields, f_v, load_sem.at[0]),
         pltpu.make_async_copy(velocity, v_v, load_sem.at[1]),
@@ -46,14 +49,8 @@
         table_load.start()
 
     barrier = pltpu.get_barrier_semaphore()
-    for o in range(1, slabs):
-        pl.semaphore_signal(
-            barrier, inc=1, device_id=(lax.rem(space + o, slabs), group), device_id_type=MESH
-        )
-    for o in range(1, groups):
-        pl.semaphore_signal(
-            barrier, inc=1, device_id=(space, lax.rem(group + o, groups)), device_id_type=MESH
-        )
+    for o in range(1, slabs * groups):
+        pl.semaphore_signal(barrier, inc=1, device_id=partner(o), device_id_type=MESH)
 
     def up(step, m):
         target = (lax.rem(space + 1, slabs), group)
@@ -86,7 +83,7 @@
     for m in range(mem):
         encode(0, m, f_v[m, depth - 1])
         e_out[0, m] = f_v[m, 0].astype(e_out.dtype)
-    pl.semaphore_wait(barrier, slabs + groups - 2)
+    pl.semaphore_wait(barrier, slabs * groups - 1)
 
     @pl.when(jnp.logical_not(last))
     def _():
@@ -220,29 +217,19 @@
         precision=HIGHEST, preferred_element_type=jnp.float32,
     )[0:1]
 
-    def copy_a(o):
-        return pltpu.make_async_remote_copy(
-            src_ref=gram_a.at[group], dst_ref=gram_a.at[group],
-            send_sem=a_send.at[o], recv_sem=a_recv.at[o],
-            device_id=(space, lax.rem(group + o, groups)), device_id_type=MESH,
-        )
+    me = space * groups + group
 
     def copy_b(o):
         return pltpu.make_async_remote_copy(
-            src_ref=gram_b.at[space], dst_ref=gram_b.at[space],
+            src_ref=gram_b.at[me], dst_ref=gram_b.at[me],
             send_sem=b_send.at[o], recv_sem=b_recv.at[o],
-            device_id=(lax.rem(space + o, slabs), group), device_id_type=MESH,
+            device_id=partner(o), device_id_type=MESH,
         )
 
-    gram_a[group] = packed
-    for o in range(1, groups):
-        copy_a(o).start()
-    for o in range(1, groups):
-        copy_a(o).wait_recv()
-    gram_b[space] = jnp.sum(gram_a[...], 0)
-    for o in range(1, slabs):
+    gram_b[me] = packed
+    for o in reversed(range(1, slabs * groups)):
         copy_b(o).start()
-    for o in range(1, slabs):
+    for o in range(1, slabs * groups):
         copy_b(o).wait_recv()
     total = jnp.sum(gram_b[...], 0) / (slabs * depth * rows * cols)
 
@@ -291,8 +278,7 @@
 
     for o in range(1, groups):
         part_copy(o).wait_send()
-        copy_a(o).wait_send()
-    for o in range(1, slabs):
+    for o in range(1, slabs * groups):
         copy_b(o).wait_send()
 
 
@@ -322,12 +308,12 @@
             vmem((STEPS, mem, 1, cols), f32), vmem((STEPS, mem, 1, cols), f32),
             vmem((STEPS, mem, rows, cols), low), vmem((STEPS, mem, rows, cols), low),
             vmem(part, low), vmem(part, low), vmem((padded, 128), f32),
-            vmem((groups, 1, padded), f32), vmem((slabs, 1, padded), f32),
+            vmem((slabs * groups, 1, padded), f32),
             dma((4,)), dma((mem, depth)),
             dma((STEPS, mem)), dma((STEPS, mem)), dma((STEPS, mem)), dma((STEPS, mem)),
             dma((STEPS, mem)), dma((STEPS, mem)),
-            dma((groups,)), dma((groups,)), dma((groups,)), dma((groups,)),
-            dma((slabs,)), dma((slabs,)),
+            dma((groups,)), dma((groups,)),
+            dma((slabs * groups,)), dma((slabs * groups,)),
         ],
         compiler_params=pltpu.CompilerParams(
             collective_id=0, has_side_effects=True, vmem_limit_bytes=64 * 1024 * 1024

time: 37.7 us -> 36.8 us (0.976)
  Pallas kernels: 33.7 us -> 32.9 us
    pallas_call x1, Pallas kernels: 33.7 us -> 32.9 us  [local(): pl.pallas_call(functools.partial(kernel, slabs, groups), out_shape=(jax.S...]
where the time goes in v3:
time: 36.8 us; the launch traced here: 36.6 us
  Pallas kernels  32.9 us (89%)
  local copies, waits for them, and re-layouts  3.13 us (9%)
  between operations  0.64 us (2%)
    pallas_call x1, Pallas kernels, local(): pl.pallas_call(functools.partial(kernel, slabs, groups), out_shape=(jax.S...  32.9 us
    unnamed x2, local copies, waits for them, and re-layouts  3.13 us

profile of v3, /device:TPU:0, one launch (start us, length us, event | category | flops | bytes accessed | tf_op | source)
XLA Modules:
  0.0 36.6 jit_solution(5761294041862789944)
XLA Ops:
  0.6 32.9 %shard_map.68 = (f32[2,2,128,256]{3,2,1,0:T(8,128)}, f32[8,8]{1,0:T(8,128)}) custom-call(s32[2]{0:T(128)} %index.1, f32[2,2,128,256]{3,2,1,0:T(8,128)} %fields.1, f32[2,128,256]{2,1,0:T(8,128)} %velocity.1, s32[2,128,256]{2,1,0:T(8,128)} %building.1, f32[32,128,256]{2,1,0:T(8,128)} %table.1), custom_call_target="tpu_custom_call" | custom-call | tf_op jit(solution)/shard_map/pallas_call | solution.py:294
  33.5 1.9 %copy.9 = f32[2,2,128,256]{3,2,1,0:T(8,128)} copy(f32[2,2,128,256]{3,2,1,0:T(8,128)} %get-tuple-element.4) | data formatting | bytes 1048576
  35.4 1.3 %copy.10 = f32[8,8]{1,0:T(8,128)} copy(f32[8,8]{1,0:T(8,128)} %get-tuple-element.5) | data formatting | bytes 512

commit v4 on v3

--- a/solution.py
+++ b/solution.py
@@ -115,11 +115,11 @@
         for m in range(mem):
             inflow[m] = t_v[index[m]]
 
-    def part_copy(o):
+    def part_copy(o, m):
         target = lax.rem(group + o, groups)
         return pltpu.make_async_remote_copy(
-            src_ref=part_out.at[target], dst_ref=part_in.at[group],
-            send_sem=part_send.at[o], recv_sem=part_recv.at[o],
+            src_ref=part_out.at[target, m], dst_ref=part_in.at[group, m],
+            send_sem=part_send.at[o, m], recv_sem=part_recv.at[o, m],
             device_id=(space, target), device_id_type=MESH,
         )
 
@@ -128,11 +128,10 @@
         pltpu.make_async_copy(u2.at[m, d], out_f.at[m, d], save_sem.at[m, d]).start()
         for i in range(per_plane):
             part_out[d * per_plane + i, m] = value[i * part_rows:(i + 1) * part_rows].astype(part_out.dtype)
-        if m == mem - 1:
-            for o in range(1, groups):
-                @pl.when(lax.rem(group + o, groups) // per_plane == d)
-                def _():
-                    part_copy(o).start()
+        for o in range(1, groups):
+            @pl.when(lax.rem(group + o, groups) // per_plane == d)
+            def _():
+                part_copy(o, m).start()
 
     old = f_v
     for step in range(STEPS):
@@ -188,7 +187,8 @@
 
     part_in[group] = part_out[group]
     for o in range(1, groups):
-        part_copy(o).wait_recv()
+        for m in range(mem):
+            part_copy(o, m).wait_recv()
 
     sums = {}
     for r in range(part_rows // 16):
@@ -277,7 +277,8 @@
                 down(step, m).wait_send()
 
     for o in range(1, groups):
-        part_copy(o).wait_send()
+        for m in range(mem):
+            part_copy(o, m).wait_send()
     for o in range(1, slabs * groups):
         copy_b(o).wait_send()
 
@@ -312,7 +313,7 @@
             dma((4,)), dma((mem, depth)),
             dma((STEPS, mem)), dma((STEPS, mem)), dma((STEPS, mem)), dma((STEPS, mem)),
             dma((STEPS, mem)), dma((STEPS, mem)),
-            dma((groups,)), dma((groups,)),
+            dma((groups, mem)), dma((groups, mem)),
             dma((slabs * groups,)), dma((slabs * groups,)),
         ],
         compiler_params=pltpu.CompilerParams(

time: 36.8 us -> 36.2 us (0.984)
  Pallas kernels: 32.9 us -> 32.2 us
    pallas_call x1, Pallas kernels: 32.9 us -> 32.2 us  [local(): pl.pallas_call(functools.partial(kernel, slabs, groups), out_shape=(jax.S...]
where the time goes in v4:
time: 36.2 us; the launch traced here: 35.9 us
  Pallas kernels  32.2 us (89%)
  local copies, waits for them, and re-layouts  3.13 us (9%)
  between operations  0.64 us (2%)
    pallas_call x1, Pallas kernels, local(): pl.pallas_call(functools.partial(kernel, slabs, groups), out_shape=(jax.S...  32.2 us
    unnamed x2, local copies, waits for them, and re-layouts  3.13 us

profile of v4, /device:TPU:0, one launch (start us, length us, event | category | flops | bytes accessed | tf_op | source)
XLA Modules:
  0.0 35.9 jit_solution(10077570743395603889)
XLA Ops:
  0.6 32.2 %shard_map.68 = (f32[2,2,128,256]{3,2,1,0:T(8,128)}, f32[8,8]{1,0:T(8,128)}) custom-call(s32[2]{0:T(128)} %index.1, f32[2,2,128,256]{3,2,1,0:T(8,128)} %fields.1, f32[2,128,256]{2,1,0:T(8,128)} %velocity.1, s32[2,128,256]{2,1,0:T(8,128)} %building.1, f32[32,128,256]{2,1,0:T(8,128)} %table.1), custom_call_target="tpu_custom_call" | custom-call | tf_op jit(solution)/shard_map/pallas_call | solution.py:295
  32.8 1.9 %copy.9 = f32[2,2,128,256]{3,2,1,0:T(8,128)} copy(f32[2,2,128,256]{3,2,1,0:T(8,128)} %get-tuple-element.4) | data formatting | bytes 1048576
  34.7 1.3 %copy.10 = f32[8,8]{1,0:T(8,128)} copy(f32[8,8]{1,0:T(8,128)} %get-tuple-element.5) | data formatting | bytes 512

commit v5 on v4

--- a/solution.py
+++ b/solution.py
@@ -85,16 +85,16 @@
         e_out[0, m] = f_v[m, 0].astype(e_out.dtype)
     pl.semaphore_wait(barrier, slabs * groups - 1)
 
+    @pl.when(jnp.logical_not(first))
+    def _():
+        for m in range(mem):
+            down(0, m).start()
+
     @pl.when(jnp.logical_not(last))
     def _():
         for m in range(mem):
             for copy in up(0, m):
                 copy.start()
-
-    @pl.when(jnp.logical_not(first))
-    def _():
-        for m in range(mem):
-            down(0, m).start()
 
     @pl.when(last)
     def _():
@@ -149,37 +149,43 @@
                 if d > 0:
                     p = p + coef_b[d] * old[m, d - 1]
                 new[m, d] = p
-        for m in range(mem):
-            @pl.when(jnp.logical_not(last))
-            def _():
-                down(step, m).wait_recv()
-
-            new[m, depth - 1] += coef_c[depth - 1] * e_in[step, m].astype(jnp.float32)
-            if step < STEPS - 1:
-                encode(step + 1, m, new[m, depth - 1])
-
+        def top(step, new):
+            for m in range(mem):
                 @pl.when(jnp.logical_not(last))
                 def _():
-                    for copy in up(step + 1, m):
-                        copy.start()
-            else:
-                finish(m, depth - 1)
-        for m in range(mem):
-            @pl.when(jnp.logical_not(first))
-            def _():
-                for copy in up(step, m):
-                    copy.wait_recv()
-                inflow[m] = w_in[step, m].astype(jnp.int32).astype(jnp.float32) * scale_in[step, m]
-
-            new[m, 0] += coef_b[0] * inflow[m]
-            if step < STEPS - 1:
-                e_out[step + 1, m] = new[m, 0].astype(e_out.dtype)
-
+                    down(step, m).wait_recv()
+
+                new[m, depth - 1] += coef_c[depth - 1] * e_in[step, m].astype(jnp.float32)
+                if step < STEPS - 1:
+                    encode(step + 1, m, new[m, depth - 1])
+
+                    @pl.when(jnp.logical_not(last))
+                    def _():
+                        for copy in up(step + 1, m):
+                            copy.start()
+                else:
+                    finish(m, depth - 1)
+
+        def bottom(step, new):
+            for m in range(mem):
                 @pl.when(jnp.logical_not(first))
                 def _():
-                    down(step + 1, m).start()
-            else:
-                finish(m, 0)
+                    for copy in up(step, m):
+                        copy.wait_recv()
+                    inflow[m] = w_in[step, m].astype(jnp.int32).astype(jnp.float32) * scale_in[step, m]
+
+                new[m, 0] += coef_b[0] * inflow[m]
+                if step < STEPS - 1:
+                    e_out[step + 1, m] = new[m, 0].astype(e_out.dtype)
+
+                    @pl.when(jnp.logical_not(first))
+                    def _():
+                        down(step + 1, m).start()
+                else:
+                    finish(m, 0)
+
+        for edge in (top, bottom) if step < STEPS - 1 else (bottom, top):
+            edge(step, new)
         old = new
     for d in range(1, depth - 1):
         for m in range(mem):

time: 36.2 us -> 38.2 us (1.055)
  Pallas kernels: 32.2 us -> 34.2 us
    pallas_call x1, Pallas kernels: 32.2 us -> 34.2 us  [local(): pl.pallas_call(functools.partial(kernel, slabs, groups), out_shape=(jax.S...]
where the time goes in v5:
time: 38.2 us; the launch traced here: 38 us
  Pallas kernels  34.2 us (90%)
  local copies, waits for them, and re-layouts  3.13 us (8%)
  between operations  0.64 us (2%)
    pallas_call x1, Pallas kernels, local(): pl.pallas_call(functools.partial(kernel, slabs, groups), out_shape=(jax.S...  34.2 us
    unnamed x2, local copies, waits for them, and re-layouts  3.13 us

profile of v5, /device:TPU:0, one launch (start us, length us, event | category | flops | bytes accessed | tf_op | source)
XLA Modules:
  0.0 38.0 jit_solution(13899238443970116855)
XLA Ops:
  0.6 34.2 %shard_map.68 = (f32[2,2,128,256]{3,2,1,0:T(8,128)}, f32[8,8]{1,0:T(8,128)}) custom-call(s32[2]{0:T(128)} %index.1, f32[2,2,128,256]{3,2,1,0:T(8,128)} %fields.1, f32[2,128,256]{2,1,0:T(8,128)} %velocity.1, s32[2,128,256]{2,1,0:T(8,128)} %building.1, f32[32,128,256]{2,1,0:T(8,128)} %table.1), custom_call_target="tpu_custom_call" | custom-call | tf_op jit(solution)/shard_map/pallas_call | solution.py:301
  34.8 1.9 %copy.9 = f32[2,2,128,256]{3,2,1,0:T(8,128)} copy(f32[2,2,128,256]{3,2,1,0:T(8,128)} %get-tuple-element.4) | data formatting | bytes 1048576
  36.7 1.3 %copy.10 = f32[8,8]{1,0:T(8,128)} copy(f32[8,8]{1,0:T(8,128)} %get-tuple-element.5) | data formatting | bytes 512
